TPU v7x, 32 devices: a whole 2x2x4 slice. The times are simulated.
32 devices in a mesh: seg: 2 (over y), tm: 4 (over x, core), state: 4 (over z).
Axes of the slice: x: 2, y: 2, z: 4, core: 2. Of those that a mesh axis runs over, the one named last changes fastest.
Arguments:
- observations: float32 [256, 512], P(('seg', 'tm')), parts along dimension 0, may hold values from -18 to 18
- gains: float32 [256, 512], P(('seg', 'tm')), parts along dimension 0, may hold values from 0.00078125 to 0.046875
- observed: int32 [256, 512], P(('seg', 'tm')), parts along dimension 0, may hold values 0 or 1
- pattern: int32 [8, 8], replicated, may hold values 0 or 1
- transition: float32 [512, 512], replicated, may hold values from -1 to 1
- initial_mean: float32 [1024], P('seg'), parts along dimension 0, may hold values from -6 to 6
Outputs:
- means: float32 [256, 512], P(('seg', 'tm'), 'state'), parts along dimension 0
There are 2 independent parts, one for each index of `seg`. A program takes and returns all parts, laid end to end along the dimension named above; an argument that names none is the same for every part. Nothing has to cross between parts.
Inputs may be any that keep to these rules, and one draw needn't show every extreme that they name: Diagonal blocks count as present whatever pattern holds there.
All inputs are finite; a program needn't handle non-finite values. No bound on the sum of `observed` on one device may be relied on, other than what follows from the above.
Results may differ from a plain program's by a relative error of at most 0.0003.
Values sent between devices are 32-bit elements; how exact they have to be, the bound alone decides.
A program may use at most 128 MiB of HBM per device.

v0:
```python
import functools

import jax
import jax.numpy as jnp
from jax import lax
from jax.experimental import pallas as pl
from jax.experimental.pallas import tpu as pltpu
from jax.sharding import PartitionSpec as P

F32 = jnp.float32
BF16 = jnp.bfloat16
VMEM = pl.BlockSpec(memory_space=pltpu.VMEM)


def split(a):
    high = a.astype(BF16)
    return high, (a - high.astype(F32)).astype(BF16)


def dot1(a, b):
    return jnp.dot(a, b, preferred_element_type=F32)


def eye_of(size):
    rows = lax.broadcasted_iota(jnp.int32, (size, size), 0)
    cols = lax.broadcasted_iota(jnp.int32, (size, size), 1)
    return (rows == cols).astype(F32)


def total(a):
    return jnp.sum(jnp.sum(a, axis=0, keepdims=True), axis=1, keepdims=True)


def build_kernel(pattern_ref, transition_ref, ft_ref, s_hi, s_lo, n_hi, x_ref, y_ref, r_ref, y_hi, y_lo):
    size = transition_ref.shape[0]
    blocks = pattern_ref.shape[0]
    block = size // blocks
    eye = functools.partial(eye_of, size)

    tall = (
        lax.broadcasted_iota(jnp.int32, (size, blocks), 0) // block
        == lax.broadcasted_iota(jnp.int32, (size, blocks), 1)
    ).astype(BF16)
    wide = (
        lax.broadcasted_iota(jnp.int32, (blocks, size), 1) // block
        == lax.broadcasted_iota(jnp.int32, (blocks, size), 0)
    ).astype(BF16)
    present = jnp.maximum(pattern_ref[...].astype(F32), eye_of(blocks)).astype(BF16)
    expand = dot1(dot1(tall, present).astype(BF16), wide)
    masked = transition_ref[...] * expand
    skew = 0.5 * (masked.T - masked)
    high, low = split(skew)
    s_hi[...] = high
    s_lo[...] = low

    normal = eye() - dot1(high, high)
    n_hi[...] = normal.astype(BF16)
    square = dot1(n_hi[...], n_hi[...])
    bound = 1.02 * jnp.sqrt(jnp.sqrt(0.5 * total(square * square)))
    bound = jnp.maximum(bound, 1.0001)

    def rescale(rho):
        worst = jnp.minimum(rho * rho, 1.0)
        return 2.0 / (2.0 - worst), worst / (2.0 - worst)

    alpha = 2.0 / (1.0 + bound)
    factor, rho = rescale((bound - 1.0) / (bound + 1.0))
    x_ref[...] = (factor * alpha) * (2.0 * eye() - alpha * normal)

    def more(carry):
        step, rho = carry
        return jnp.logical_and(jnp.max(rho) > 0.03, step < 24)

    def newton(carry):
        step, rho = carry
        x_hi = x_ref[...].astype(BF16)
        res = eye() - dot1(n_hi[...], x_hi)
        factor, rho = rescale(rho)
        x_ref[...] = factor * (x_ref[...] + dot1(x_hi, res.astype(BF16)))
        return step + 1, rho

    lax.while_loop(more, newton, (0, rho))
    y_ref[...] = x_ref[...] + dot1(x_ref[...].astype(BF16), s_hi[...])

    def residual():
        high, low = split(y_ref[...])
        y_hi[...] = high
        y_lo[...] = low
        prod = dot1(s_hi[...], y_lo[...]) + dot1(s_lo[...], y_hi[...])
        res = eye() - y_ref[...] + (prod + dot1(s_hi[...], y_hi[...]))
        r_ref[...] = res
        return jnp.max(total(res * res))

    first = residual()
    good = first < 0.5

    @pl.when(jnp.logical_not(good))
    def _():
        y_ref[...] = (1.9 / (1.0 + bound)) * (
            eye() + (s_hi[...].astype(F32) + s_lo[...].astype(F32))
        )
        residual()

    def unfinished(carry):
        step, size2 = carry
        return jnp.logical_and(jnp.logical_not(size2 < 6e-5), step < 64)

    def refine(carry):
        step, unused = carry
        r_hi, r_lo = split(r_ref[...])
        prod = dot1(y_hi[...], r_lo) + dot1(y_lo[...], r_hi)
        y_ref[...] += prod + dot1(y_hi[...], r_hi)
        return step + 1, residual()

    lax.while_loop(unfinished, refine, (0, jnp.where(good, first, 1e9)))
    last = y_ref[...] + dot1(y_hi[...], r_ref[...].astype(BF16))
    ft_ref[...] = 2.0 * last - eye()


def build(pattern, transition):
    size = transition.shape[0]
    square = (size, size)
    return pl.pallas_call(
        build_kernel,
        out_shape=jax.ShapeDtypeStruct(square, F32),
        in_specs=[VMEM, VMEM],
        out_specs=VMEM,
        scratch_shapes=[
            pltpu.VMEM(square, BF16),
            pltpu.VMEM(square, BF16),
            pltpu.VMEM(square, BF16),
            pltpu.VMEM(square, F32),
            pltpu.VMEM(square, F32),
            pltpu.VMEM(square, F32),
            pltpu.VMEM(square, BF16),
            pltpu.VMEM(square, BF16),
        ],
        compiler_params=pltpu.CompilerParams(vmem_limit_bytes=40 << 20),
        cost_estimate=pl.CostEstimate(
            flops=40 * size**3, bytes_accessed=8 * size**2, transcendentals=0
        ),
        name="build_transition",
    )(pattern, transition)


def scan_kernel(ft_ref, frames_ref, start_ref, out_ref, kept):
    size = ft_ref.shape[0]
    frames, width = out_ref.shape
    mine = lax.axis_index("tm")
    offset = 0 if width == size else lax.axis_index("state") * width

    def step(t, row):
        acc = [jnp.zeros((8, size), F32), jnp.zeros((8, size), F32)]
        for tile in range(size // 128):
            piece = row[:, 128 * tile : 128 * tile + 128]
            column = jnp.broadcast_to(piece, (128, 128)).T
            for group in range(16):
                at = 128 * tile + 8 * group
                spread = jnp.concatenate([column[8 * group : 8 * group + 8]] * (size // 128), 1)
                acc[group % 2] += ft_ref[at : at + 8, :] * spread
        moved = jnp.sum(acc[0] + acc[1], axis=0, keepdims=True)
        damp = frames_ref[pl.ds(t, 1), pl.ds(0, size)]
        drive = frames_ref[pl.ds(t, 1), pl.ds(size, size)]
        row = damp * moved + drive
        kept[pl.ds(t, 1), :] = row
        return row

    lax.fori_loop(0, (mine + 1) * frames, step, start_ref[...])
    out_ref[...] = kept[
        pl.ds(pl.multiple_of(mine * frames, frames), frames),
        pl.ds(0, size) if width == size else pl.ds(pl.multiple_of(offset, width), width),
    ]


def body(observations, gains, observed, pattern, transition, initial_mean):
    frames, size = observations.shape
    width = size // lax.axis_size("state")
    seen = gains * observed.astype(F32)
    packed = jnp.concatenate([1.0 - seen, seen * observations], axis=1)
    packed = lax.all_gather(packed, "tm", axis=0, tiled=True)
    ft = build(pattern, transition)
    kept_width = width if width % 128 == 0 else size
    means = pl.pallas_call(
        scan_kernel,
        out_shape=jax.ShapeDtypeStruct((frames, kept_width), F32),
        in_specs=[VMEM, VMEM, VMEM],
        out_specs=VMEM,
        scratch_shapes=[pltpu.VMEM((packed.shape[0], size), F32)],
        compiler_params=pltpu.CompilerParams(vmem_limit_bytes=40 << 20),
        name="scan_frames",
    )(ft, packed, initial_mean.reshape(1, size))
    if kept_width == width:
        return means
    return lax.dynamic_slice_in_dim(means, lax.axis_index("state") * width, width, 1)


def solution(mesh):
    return jax.shard_map(
        body,
        mesh=mesh,
        in_specs=(
            P(("seg", "tm"), None),
            P(("seg", "tm"), None),
            P(("seg", "tm"), None),
            P(),
            P(),
            P("seg"),
        ),
        out_specs=P(("seg", "tm"), "state"),
        check_vma=False,
    )
```

profile of v0, /device:TPU:27, one launch (start us, length us, event | category | flops | bytes accessed | tf_op | source)
XLA Modules:
  0.0 38.0 jit_solution(8373740090787779319)
XLA Ops:
  0.0 0.0 copy-start.1
  0.0 1.0 %broadcast_subtract_fusion = (f32[32,512]{1,0:T(8,128)S(1)}, f32[32,512]{1,0:T(8,128)S(1)}) fusion(f32[32,512]{1,0:T(8,128)} %param.7, s32[32,512]{1,0:T(8,128)} %param.8, f32[32,512]{1,0:T(8,128)} %param.6), kind=kLoop, calls=%fused_computation.2 | loop fusion | flops 65536 | bytes 327680 | tf_op jit(solution)/shard_map/sub | solution.py:179
  1.0 0.0 copy-start.2
  1.0 7.3 %all_gather.3.frames_ref = f32[128,1024]{1,0:T(8,128)S(1)} all-gather(f32[32,1024]{1,0:T(8,128)S(1)} %pad_maximum_fusion), channel_id=1, replica_groups=mesh['seg'=2,'tm'=4,'state'=4] {'tm'}, dimensions={0}, use_global_device_ids=true | all-gather | bytes 655360 | tf_op jit(solution)/shard_map/all_gather | solution.py:180
  8.3 0.0 copy-done.1
  8.3 0.0 copy-done.2
  8.3 0.0 copy-start
  8.3 8.0 %build_transition.1.ft_ref = f32[512,512]{1,0:T(8,128)S(1)} custom-call(s32[8,8]{1,0:T(8,128)S(1)} %copy-done.2, f32[512,512]{1,0:T(8,128)S(1)} %copy-done.1), custom_call_target="tpu_custom_call" | custom-call | flops 5368709120 | bytes 2097152 | tf_op jit(solution)/shard_map/build_transition/pallas_call | solution.py:123
  16.3 0.0 copy-done
  16.3 21.7 %scan_frames.1 = f32[32,128]{1,0:T(8,128)} custom-call(f32[512,512]{1,0:T(8,128)S(1)} %build_transition.1.ft_ref, f32[128,1024]{1,0:T(8,128)S(1)} %all_gather.3.frames_ref, f32[1,512]{1,0:T(1,128)S(1)} %bitcast.1), custom_call_target="tpu_custom_call" | custom-call | tf_op jit(solution)/shard_map/scan_frames/pallas_call | solution.py:183
  (1 shorter events, 0.0 us)
Async XLA Ops:
  0.0 8.3 %copy-start.1 = (f32[512,512]{1,0:T(8,128)S(1)}, f32[512,512]{1,0:T(8,128)}, u32[]{:S(2)}) copy-start(f32[512,512]{1,0:T(8,128)} %transition_ref.1) | copy-start | bytes 3145732
  1.0 7.3 %copy-start.2 = (s32[8,8]{1,0:T(8,128)S(1)}, s32[8,8]{1,0:T(8,128)}, u32[]{:S(2)}) copy-start(s32[8,8]{1,0:T(8,128)} %pattern_ref.1) | copy-start | bytes 772
  8.3 8.0 %copy-start = (f32[512]{0:T(512)S(1)}, f32[512]{0:T(512)}, u32[]{:S(2)}) copy-start(f32[512]{0:T(512)} %param.11) | copy-start | bytes 6148
where the time goes:
time: 38.2 us; the launch traced here: 38 us
  Pallas kernels  29.7 us (78%)
  blocking collectives  7.29 us (19%)
  other arithmetic  1.02 us (3%)
    pallas_call x1, Pallas kernels, body(): pl.pallas_call(scan_kernel, out_shape=jax.ShapeDtypeStruct((frames, kept_...  21.7 us
    pallas_call x1, Pallas kernels, build(): pl.pallas_call(build_kernel, out_shape=jax.ShapeDtypeStruct(square, F32),...  7.95 us
    all_gather x1, blocking collectives, body(): packed = lax.all_gather(packed, 'tm', axis=0, tiled=True)  7.29 us
    sub x1, other arithmetic, body(): packed = jnp.concatenate([1.0 - seen, seen * observations], axis=1)  1.01 us

commit v1 on v0

--- a/solution.py
+++ b/solution.py
@@ -10,6 +10,8 @@
 F32 = jnp.float32
 BF16 = jnp.bfloat16
 VMEM = pl.BlockSpec(memory_space=pltpu.VMEM)
+MESH = pl.DeviceIdType.MESH
+NEWTON_STEPS = 3
 
 
 def split(a):
@@ -31,11 +33,40 @@
     return jnp.sum(jnp.sum(a, axis=0, keepdims=True), axis=1, keepdims=True)
 
 
-def build_kernel(pattern_ref, transition_ref, ft_ref, s_hi, s_lo, n_hi, x_ref, y_ref, r_ref, y_hi, y_lo):
+def share_and_build_kernel(
+    observations_ref, gains_ref, observed_ref, pattern_ref, transition_ref,
+    y_ref, s_hi, s_lo, packed_ref,
+    own, slots, n_hi, x_ref, send_sem, recv_sem,
+):
     size = transition_ref.shape[0]
     blocks = pattern_ref.shape[0]
     block = size // blocks
+    frames = observations_ref.shape[0]
+    count = slots.shape[0]
+    mine = lax.axis_index("tm")
     eye = functools.partial(eye_of, size)
+
+    barrier = pltpu.get_barrier_semaphore()
+    for hop in range(1, count):
+        pl.semaphore_signal(
+            barrier, inc=1, device_id={"tm": lax.rem(mine + hop, count)}, device_id_type=MESH
+        )
+    seen = gains_ref[...] * observed_ref[...].astype(F32)
+    own[:, :size] = 1.0 - seen
+    own[:, size:] = seen * observations_ref[...]
+    pl.semaphore_wait(barrier, count - 1)
+    copies = []
+    for hop in range(1, count):
+        copy = pltpu.make_async_remote_copy(
+            src_ref=own,
+            dst_ref=slots.at[mine],
+            send_sem=send_sem.at[hop],
+            recv_sem=recv_sem.at[hop],
+            device_id={"tm": lax.rem(mine + hop, count)},
+            device_id_type=MESH,
+        )
+        copy.start()
+        copies.append(copy)
 
     tall = (
         lax.broadcasted_iota(jnp.int32, (size, blocks), 0) // block
@@ -67,38 +98,83 @@
     factor, rho = rescale((bound - 1.0) / (bound + 1.0))
     x_ref[...] = (factor * alpha) * (2.0 * eye() - alpha * normal)
 
-    def more(carry):
-        step, rho = carry
-        return jnp.logical_and(jnp.max(rho) > 0.03, step < 24)
-
-    def newton(carry):
-        step, rho = carry
+    def newton(step, rho):
         x_hi = x_ref[...].astype(BF16)
         res = eye() - dot1(n_hi[...], x_hi)
         factor, rho = rescale(rho)
         x_ref[...] = factor * (x_ref[...] + dot1(x_hi, res.astype(BF16)))
-        return step + 1, rho
-
-    lax.while_loop(more, newton, (0, rho))
+        return rho
+
+    lax.fori_loop(0, NEWTON_STEPS, newton, rho)
     y_ref[...] = x_ref[...] + dot1(x_ref[...].astype(BF16), s_hi[...])
 
+    for copy in copies:
+        copy.wait_recv()
+    for place in range(count):
+        rows = pl.ds(place * frames, frames)
+
+        @pl.when(mine == place)
+        def _():
+            packed_ref[rows, :] = own[...]
+
+        @pl.when(mine != place)
+        def _():
+            packed_ref[rows, :] = slots[place]
+
+    for copy in copies:
+        copy.wait_send()
+
+
+def share_and_build(observations, gains, observed, pattern, transition):
+    frames, size = observations.shape
+    count = lax.axis_size("tm")
+    square = (size, size)
+    return pl.pallas_call(
+        share_and_build_kernel,
+        out_shape=(
+            jax.ShapeDtypeStruct(square, F32),
+            jax.ShapeDtypeStruct(square, BF16),
+            jax.ShapeDtypeStruct(square, BF16),
+            jax.ShapeDtypeStruct((count * frames, 2 * size), F32),
+        ),
+        in_specs=[VMEM] * 5,
+        out_specs=(VMEM,) * 4,
+        scratch_shapes=[
+            pltpu.VMEM((frames, 2 * size), F32),
+            pltpu.VMEM((count, frames, 2 * size), F32),
+            pltpu.VMEM(square, BF16),
+            pltpu.VMEM(square, F32),
+            pltpu.SemaphoreType.DMA((count,)),
+            pltpu.SemaphoreType.DMA((count,)),
+        ],
+        compiler_params=pltpu.CompilerParams(
+            vmem_limit_bytes=40 << 20, collective_id=0, has_side_effects=True
+        ),
+        name="share_and_build",
+    )(observations, gains, observed, pattern, transition)
+
+
+def refine_to_transition(y_ref, s_hi, s_lo, ft_ref, r_ref, y_hi, y_lo):
+    size = y_ref.shape[0]
+    eye = functools.partial(eye_of, size)
+
     def residual():
-        high, low = split(y_ref[...])
+        high, low = split(ft_ref[...])
         y_hi[...] = high
         y_lo[...] = low
         prod = dot1(s_hi[...], y_lo[...]) + dot1(s_lo[...], y_hi[...])
-        res = eye() - y_ref[...] + (prod + dot1(s_hi[...], y_hi[...]))
+        res = eye() - ft_ref[...] + (prod + dot1(s_hi[...], y_hi[...]))
         r_ref[...] = res
         return jnp.max(total(res * res))
 
+    ft_ref[...] = y_ref[...]
     first = residual()
     good = first < 0.5
 
     @pl.when(jnp.logical_not(good))
     def _():
-        y_ref[...] = (1.9 / (1.0 + bound)) * (
-            eye() + (s_hi[...].astype(F32) + s_lo[...].astype(F32))
-        )
+        skew = s_hi[...].astype(F32) + s_lo[...].astype(F32)
+        ft_ref[...] = (1.9 / (2.0 + total(skew * skew))) * (eye() + skew)
         residual()
 
     def unfinished(carry):
@@ -109,41 +185,16 @@
         step, unused = carry
         r_hi, r_lo = split(r_ref[...])
         prod = dot1(y_hi[...], r_lo) + dot1(y_lo[...], r_hi)
-        y_ref[...] += prod + dot1(y_hi[...], r_hi)
+        ft_ref[...] += prod + dot1(y_hi[...], r_hi)
         return step + 1, residual()
 
     lax.while_loop(unfinished, refine, (0, jnp.where(good, first, 1e9)))
-    last = y_ref[...] + dot1(y_hi[...], r_ref[...].astype(BF16))
+    last = ft_ref[...] + dot1(y_hi[...], r_ref[...].astype(BF16))
     ft_ref[...] = 2.0 * last - eye()
 
 
-def build(pattern, transition):
-    size = transition.shape[0]
-    square = (size, size)
-    return pl.pallas_call(
-        build_kernel,
-        out_shape=jax.ShapeDtypeStruct(square, F32),
-        in_specs=[VMEM, VMEM],
-        out_specs=VMEM,
-        scratch_shapes=[
-            pltpu.VMEM(square, BF16),
-            pltpu.VMEM(square, BF16),
-            pltpu.VMEM(square, BF16),
-            pltpu.VMEM(square, F32),
-            pltpu.VMEM(square, F32),
-            pltpu.VMEM(square, F32),
-            pltpu.VMEM(square, BF16),
-            pltpu.VMEM(square, BF16),
-        ],
-        compiler_params=pltpu.CompilerParams(vmem_limit_bytes=40 << 20),
-        cost_estimate=pl.CostEstimate(
-            flops=40 * size**3, bytes_accessed=8 * size**2, transcendentals=0
-        ),
-        name="build_transition",
-    )(pattern, transition)
-
-
-def scan_kernel(ft_ref, frames_ref, start_ref, out_ref, kept):
+def scan_kernel(y_ref, s_hi, s_lo, frames_ref, start_ref, out_ref, ft_ref, r_ref, y_hi, y_lo, kept):
+    refine_to_transition(y_ref, s_hi, s_lo, ft_ref, r_ref, y_hi, y_lo)
     size = ft_ref.shape[0]
     frames, width = out_ref.shape
     mine = lax.axis_index("tm")
@@ -175,20 +226,26 @@
 def body(observations, gains, observed, pattern, transition, initial_mean):
     frames, size = observations.shape
     width = size // lax.axis_size("state")
-    seen = gains * observed.astype(F32)
-    packed = jnp.concatenate([1.0 - seen, seen * observations], axis=1)
-    packed = lax.all_gather(packed, "tm", axis=0, tiled=True)
-    ft = build(pattern, transition)
+    start, s_hi, s_lo, packed = share_and_build(
+        observations, gains, observed, pattern, transition
+    )
     kept_width = width if width % 128 == 0 else size
+    square = (size, size)
     means = pl.pallas_call(
         scan_kernel,
         out_shape=jax.ShapeDtypeStruct((frames, kept_width), F32),
-        in_specs=[VMEM, VMEM, VMEM],
+        in_specs=[VMEM] * 5,
         out_specs=VMEM,
-        scratch_shapes=[pltpu.VMEM((packed.shape[0], size), F32)],
+        scratch_shapes=[
+            pltpu.VMEM(square, F32),
+            pltpu.VMEM(square, F32),
+            pltpu.VMEM(square, BF16),
+            pltpu.VMEM(square, BF16),
+            pltpu.VMEM((packed.shape[0], size), F32),
+        ],
         compiler_params=pltpu.CompilerParams(vmem_limit_bytes=40 << 20),
-        name="scan_frames",
-    )(ft, packed, initial_mean.reshape(1, size))
+        name="refine_and_scan",
+    )(start, s_hi, s_lo, packed, initial_mean.reshape(1, size))
     if kept_width == width:
         return means
     return lax.dynamic_slice_in_dim(means, lax.axis_index("state") * width, width, 1)

time: 38.2 us -> 39.2 us (1.026)
  blocking collectives: 7.29 us -> 0 us
  local copies, waits for them, and re-layouts: 0.01 us -> 5.1 us
  Pallas kernels: 29.7 us -> 33.8 us
  other arithmetic: 1.02 us -> 0 us
    all_gather x1 -> x0, blocking collectives: 7.29 us -> none  [body(): packed = lax.all_gather(packed, 'tm', axis=0, tiled=True)]
    unnamed x6 -> x12, local copies, waits for them, and re-layouts: 0.01 us -> 5.1 us
    pallas_call x1, Pallas kernels: 21.7 us -> 25 us  [body(): pl.pallas_call(scan_kernel, out_shape=jax.ShapeDtypeStruct((frames, kept_...]
    sub x1 -> x0, other arithmetic: 1.01 us -> none  [body(): packed = jnp.concatenate([1.0 - seen, seen * observations], axis=1)]
    pallas_call x1, Pallas kernels: 7.95 us -> 8.77 us  [share_and_build(): pl.pallas_call(share_and_build_kernel, out_shape=(jax.ShapeDtypeStruct(sq...]
where the time goes in v1:
time: 39.2 us; the launch traced here: 38.9 us
  Pallas kernels  33.8 us (86%)
  local copies, waits for them, and re-layouts  5.1 us (13%)
    pallas_call x1, Pallas kernels, body(): pl.pallas_call(scan_kernel, out_shape=jax.ShapeDtypeStruct((frames, kept_...  25 us
    pallas_call x1, Pallas kernels, share_and_build(): pl.pallas_call(share_and_build_kernel, out_shape=(jax.ShapeDtypeStruct(sq...  8.77 us
    unnamed x12, local copies, waits for them, and re-layouts  5.1 us

profile of v1, /device:TPU:27, one launch (start us, length us, event | category | flops | bytes accessed | tf_op | source)
XLA Modules:
  0.0 38.9 jit_solution(12718984642679408825)
XLA Ops:
  0.0 0.0 copy-start
  0.0 1.2 %copy-done = f32[512,512]{1,0:T(8,128)S(1)} copy-done((f32[512,512]{1,0:T(8,128)S(1)}, f32[512,512]{1,0:T(8,128)}, u32[]{:S(2)}) %copy-start) | copy-done | bytes 1048600
  1.2 0.0 copy-start.1
  1.2 0.8 %copy-done.1 = f32[32,512]{1,0:T(8,128)S(1)} copy-done((f32[32,512]{1,0:T(8,128)S(1)}, f32[32,512]{1,0:T(8,128)}, u32[]{:S(2)}) %copy-start.1) | copy-done | bytes 65560
  2.1 0.0 copy-start.2
  2.1 0.8 %copy-done.2 = f32[32,512]{1,0:T(8,128)S(1)} copy-done((f32[32,512]{1,0:T(8,128)S(1)}, f32[32,512]{1,0:T(8,128)}, u32[]{:S(2)}) %copy-start.2) | copy-done | bytes 65560
  2.9 0.0 copy-start.3
  2.9 0.8 %copy-done.3 = s32[32,512]{1,0:T(8,128)S(1)} copy-done((s32[32,512]{1,0:T(8,128)S(1)}, s32[32,512]{1,0:T(8,128)}, u32[]{:S(2)}) %copy-start.3) | copy-done | bytes 65560
  3.7 0.0 copy-start.4
  3.7 0.7 %copy-done.4 = s32[8,8]{1,0:T(8,128)S(1)} copy-done((s32[8,8]{1,0:T(8,128)S(1)}, s32[8,8]{1,0:T(8,128)}, u32[]{:S(2)}) %copy-start.4) | copy-done | bytes 280
  4.4 8.8 %share_and_build.1 = (f32[512,512]{1,0:T(8,128)S(1)}, bf16[512,512]{1,0:T(8,128)(2,1)S(1)}, bf16[512,512]{1,0:T(8,128)(2,1)S(1)}, f32[128,1024]{1,0:T(8,128)S(1)}) custom-call(f32[32,512]{1,0:T(8,128)S(1)} %copy-done.1, f32[32,512]{1,0:T(8,128)S(1)} %copy-done.2, s32[32,512]{1,0:T(8,128)S(1)} %copy-done.3, s32[8,8]{1,0:T(8,128)S(1)} %copy-done.4, ...), custom_call_target="tpu_custom_call" | custom-call | tf_op jit(solution)/shard_map/share_and_build/pallas_call | solution.py:132
  13.2 0.0 copy-start.5
  13.2 0.7 %copy-done.5 = f32[512]{0:T(512)S(1)} copy-done((f32[512]{0:T(512)S(1)}, f32[512]{0:T(512)}, u32[]{:S(2)}) %copy-start.5) | copy-done | bytes 2072
  13.9 25.0 %refine_and_scan.1 = f32[32,128]{1,0:T(8,128)} custom-call(f32[512,512]{1,0:T(8,128)S(1)} %get-tuple-element.9.y_ref, bf16[512,512]{1,0:T(8,128)(2,1)S(1)} %get-tuple-element.10.s_hi, bf16[512,512]{1,0:T(8,128)(2,1)S(1)} %get-tuple-element.11.s_lo, f32[128,1024]{1,0:T(8,128)S(1)} %get-tuple-element.12.frames_ref, f32[1,512]{1,0:T(1,128)S(1)} %bitcast.1), custom_call_target="tpu_custom_call" | custom-call | tf_op jit(solution)/shard_map/refine_and_scan/pallas_call | solution.py:234
Async XLA Ops:
  0.0 1.2 %copy-start = (f32[512,512]{1,0:T(8,128)S(1)}, f32[512,512]{1,0:T(8,128)}, u32[]{:S(2)}) copy-start(f32[512,512]{1,0:T(8,128)} %transition_ref.1) | copy-start | bytes 3145732
  1.2 0.8 %copy-start.1 = (f32[32,512]{1,0:T(8,128)S(1)}, f32[32,512]{1,0:T(8,128)}, u32[]{:S(2)}) copy-start(f32[32,512]{1,0:T(8,128)} %observations_ref.1) | copy-start | bytes 196612
  2.1 0.8 %copy-start.2 = (f32[32,512]{1,0:T(8,128)S(1)}, f32[32,512]{1,0:T(8,128)}, u32[]{:S(2)}) copy-start(f32[32,512]{1,0:T(8,128)} %gains_ref.1) | copy-start | bytes 196612
  2.9 0.8 %copy-start.3 = (s32[32,512]{1,0:T(8,128)S(1)}, s32[32,512]{1,0:T(8,128)}, u32[]{:S(2)}) copy-start(s32[32,512]{1,0:T(8,128)} %observed_ref.1) | copy-start | bytes 196612
  3.7 0.7 %copy-start.4 = (s32[8,8]{1,0:T(8,128)S(1)}, s32[8,8]{1,0:T(8,128)}, u32[]{:S(2)}) copy-start(s32[8,8]{1,0:T(8,128)} %pattern_ref.1) | copy-start | bytes 772
  13.2 0.7 %copy-start.5 = (f32[512]{0:T(512)S(1)}, f32[512]{0:T(512)}, u32[]{:S(2)}) copy-start(f32[512]{0:T(512)} %param.11) | copy-start | bytes 6148

commit v2 on v1

--- a/solution.py
+++ b/solution.py
@@ -10,6 +10,7 @@
 F32 = jnp.float32
 BF16 = jnp.bfloat16
 VMEM = pl.BlockSpec(memory_space=pltpu.VMEM)
+HBM = pl.BlockSpec(memory_space=pltpu.HBM)
 MESH = pl.DeviceIdType.MESH
 NEWTON_STEPS = 3
 
@@ -34,10 +35,22 @@
 
 
 def share_and_build_kernel(
+    observations_hbm, gains_hbm, observed_hbm, pattern_hbm, transition_hbm,
+    y_hbm, s_hi_hbm, s_lo_hbm, packed_hbm,
+    y_ref, s_hi, s_lo,
     observations_ref, gains_ref, observed_ref, pattern_ref, transition_ref,
-    y_ref, s_hi, s_lo, packed_ref,
-    own, slots, n_hi, x_ref, send_sem, recv_sem,
+    own, slots, n_hi, x_ref, load_sem, save_sem, send_sem, recv_sem,
 ):
+    loads = []
+    for place, (source, target) in enumerate((
+        (observations_hbm, observations_ref),
+        (gains_hbm, gains_ref),
+        (observed_hbm, observed_ref),
+        (pattern_hbm, pattern_ref),
+        (transition_hbm, transition_ref),
+    )):
+        loads.append(pltpu.make_async_copy(source, target, load_sem.at[place]))
+        loads[-1].start()
     size = transition_ref.shape[0]
     blocks = pattern_ref.shape[0]
     block = size // blocks
@@ -46,28 +59,42 @@
     mine = lax.axis_index("tm")
     eye = functools.partial(eye_of, size)
 
+    chips = count // 2
+    core = lax.rem(mine, 2)
+    chip = mine // 2
+    partner = {"tm": 2 * chip + 1 - core}
+    others = [2 * lax.rem(chip + hop, chips) + core for hop in range(1, chips)]
+    sources = [2 * lax.rem(chip + chips - hop, chips) + core for hop in range(1, chips)]
+
     barrier = pltpu.get_barrier_semaphore()
-    for hop in range(1, count):
-        pl.semaphore_signal(
-            barrier, inc=1, device_id={"tm": lax.rem(mine + hop, count)}, device_id_type=MESH
-        )
+    for target in [partner] + [{"tm": other} for other in others]:
+        pl.semaphore_signal(barrier, inc=1, device_id=target, device_id_type=MESH)
+    for load in loads[:3]:
+        load.wait()
     seen = gains_ref[...] * observed_ref[...].astype(F32)
     own[:, :size] = 1.0 - seen
     own[:, size:] = seen * observations_ref[...]
-    pl.semaphore_wait(barrier, count - 1)
-    copies = []
-    for hop in range(1, count):
+    pl.semaphore_wait(barrier, chips)
+
+    def send(source, place, target, sem):
         copy = pltpu.make_async_remote_copy(
-            src_ref=own,
-            dst_ref=slots.at[mine],
-            send_sem=send_sem.at[hop],
-            recv_sem=recv_sem.at[hop],
-            device_id={"tm": lax.rem(mine + hop, count)},
+            src_ref=source,
+            dst_ref=slots.at[place],
+            send_sem=send_sem.at[sem],
+            recv_sem=recv_sem.at[sem],
+            device_id=target,
             device_id_type=MESH,
         )
         copy.start()
-        copies.append(copy)
-
+        return copy
+
+    direct = [
+        send(own, mine, {"tm": other}, hop) for hop, other in enumerate(others, 1)
+    ]
+    passed = [send(own, mine, partner, 0)]
+
+    for load in loads[3:]:
+        load.wait()
     tall = (
         lax.broadcasted_iota(jnp.int32, (size, blocks), 0) // block
         == lax.broadcasted_iota(jnp.int32, (size, blocks), 1)
@@ -83,6 +110,12 @@
     high, low = split(skew)
     s_hi[...] = high
     s_lo[...] = low
+    saves = [
+        pltpu.make_async_copy(s_hi, s_hi_hbm, save_sem.at[0]),
+        pltpu.make_async_copy(s_lo, s_lo_hbm, save_sem.at[1]),
+    ]
+    for save in saves:
+        save.start()
 
     normal = eye() - dot1(high, high)
     n_hi[...] = normal.astype(BF16)
@@ -105,23 +138,23 @@
         x_ref[...] = factor * (x_ref[...] + dot1(x_hi, res.astype(BF16)))
         return rho
 
-    lax.fori_loop(0, NEWTON_STEPS, newton, rho)
+    rho = lax.fori_loop(0, NEWTON_STEPS - 1, newton, rho)
+    for hop, source in enumerate(sources, 1):
+        direct[hop - 1].wait_recv()
+        passed.append(send(slots.at[source], source, partner, chips + hop))
+    newton(0, rho)
     y_ref[...] = x_ref[...] + dot1(x_ref[...].astype(BF16), s_hi[...])
 
-    for copy in copies:
+    saves.append(pltpu.make_async_copy(y_ref, y_hbm, save_sem.at[2]))
+    saves[-1].start()
+    for copy in passed:
         copy.wait_recv()
-    for place in range(count):
-        rows = pl.ds(place * frames, frames)
-
-        @pl.when(mine == place)
-        def _():
-            packed_ref[rows, :] = own[...]
-
-        @pl.when(mine != place)
-        def _():
-            packed_ref[rows, :] = slots[place]
-
-    for copy in copies:
+    slots[mine] = own[...]
+    saves.append(pltpu.make_async_copy(slots, packed_hbm, save_sem.at[3]))
+    saves[-1].start()
+    for save in saves:
+        save.wait()
+    for copy in direct + passed:
         copy.wait_send()
 
 
@@ -135,27 +168,37 @@
             jax.ShapeDtypeStruct(square, F32),
             jax.ShapeDtypeStruct(square, BF16),
             jax.ShapeDtypeStruct(square, BF16),
-            jax.ShapeDtypeStruct((count * frames, 2 * size), F32),
+            jax.ShapeDtypeStruct((count, frames, 2 * size), F32),
         ),
-        in_specs=[VMEM] * 5,
-        out_specs=(VMEM,) * 4,
+        in_specs=[HBM] * 5,
+        out_specs=(HBM,) * 4,
         scratch_shapes=[
+            pltpu.VMEM(square, F32),
+            pltpu.VMEM(square, BF16),
+            pltpu.VMEM(square, BF16),
+            pltpu.VMEM((frames, size), F32),
+            pltpu.VMEM((frames, size), F32),
+            pltpu.VMEM((frames, size), jnp.int32),
+            pltpu.VMEM(pattern.shape, jnp.int32),
+            pltpu.VMEM(square, F32),
             pltpu.VMEM((frames, 2 * size), F32),
             pltpu.VMEM((count, frames, 2 * size), F32),
             pltpu.VMEM(square, BF16),
             pltpu.VMEM(square, F32),
+            pltpu.SemaphoreType.DMA((5,)),
+            pltpu.SemaphoreType.DMA((4,)),
             pltpu.SemaphoreType.DMA((count,)),
             pltpu.SemaphoreType.DMA((count,)),
         ],
         compiler_params=pltpu.CompilerParams(
-            vmem_limit_bytes=40 << 20, collective_id=0, has_side_effects=True
+            vmem_limit_bytes=60 << 20, collective_id=0, has_side_effects=True
         ),
         name="share_and_build",
     )(observations, gains, observed, pattern, transition)
 
 
-def refine_to_transition(y_ref, s_hi, s_lo, ft_ref, r_ref, y_hi, y_lo):
-    size = y_ref.shape[0]
+def refine_to_transition(s_hi, s_lo, ft_ref, r_ref, y_hi, y_lo):
+    size = ft_ref.shape[0]
     eye = functools.partial(eye_of, size)
 
     def residual():
@@ -167,7 +210,6 @@
         r_ref[...] = res
         return jnp.max(total(res * res))
 
-    ft_ref[...] = y_ref[...]
     first = residual()
     good = first < 0.5
 
@@ -193,8 +235,25 @@
     ft_ref[...] = 2.0 * last - eye()
 
 
-def scan_kernel(y_ref, s_hi, s_lo, frames_ref, start_ref, out_ref, ft_ref, r_ref, y_hi, y_lo, kept):
-    refine_to_transition(y_ref, s_hi, s_lo, ft_ref, r_ref, y_hi, y_lo)
+def scan_kernel(
+    y_hbm, s_hi_hbm, s_lo_hbm, frames_hbm, start_hbm, out_ref,
+    ft_ref, s_hi, s_lo, frames_ref, start_ref, r_ref, y_hi, y_lo, kept, load_sem,
+):
+    loads = []
+    for place, (source, target) in enumerate((
+        (y_hbm, ft_ref),
+        (s_hi_hbm, s_hi),
+        (s_lo_hbm, s_lo),
+        (frames_hbm, frames_ref),
+        (start_hbm, start_ref),
+    )):
+        loads.append(pltpu.make_async_copy(source, target, load_sem.at[place]))
+        loads[-1].start()
+    for load in loads[:3]:
+        load.wait()
+    refine_to_transition(s_hi, s_lo, ft_ref, r_ref, y_hi, y_lo)
+    for load in loads[3:]:
+        load.wait()
     size = ft_ref.shape[0]
     frames, width = out_ref.shape
     mine = lax.axis_index("tm")
@@ -210,8 +269,8 @@
                 spread = jnp.concatenate([column[8 * group : 8 * group + 8]] * (size // 128), 1)
                 acc[group % 2] += ft_ref[at : at + 8, :] * spread
         moved = jnp.sum(acc[0] + acc[1], axis=0, keepdims=True)
-        damp = frames_ref[pl.ds(t, 1), pl.ds(0, size)]
-        drive = frames_ref[pl.ds(t, 1), pl.ds(size, size)]
+        damp = frames_ref[pl.ds(t, 1), :size]
+        drive = frames_ref[pl.ds(t, 1), size:]
         row = damp * moved + drive
         kept[pl.ds(t, 1), :] = row
         return row
@@ -229,21 +288,27 @@
     start, s_hi, s_lo, packed = share_and_build(
         observations, gains, observed, pattern, transition
     )
+    packed = packed.reshape(-1, 2 * size)
     kept_width = width if width % 128 == 0 else size
     square = (size, size)
     means = pl.pallas_call(
         scan_kernel,
         out_shape=jax.ShapeDtypeStruct((frames, kept_width), F32),
-        in_specs=[VMEM] * 5,
+        in_specs=[HBM] * 5,
         out_specs=VMEM,
         scratch_shapes=[
             pltpu.VMEM(square, F32),
+            pltpu.VMEM(square, BF16),
+            pltpu.VMEM(square, BF16),
+            pltpu.VMEM((packed.shape[0], 2 * size), F32),
+            pltpu.VMEM((1, size), F32),
             pltpu.VMEM(square, F32),
             pltpu.VMEM(square, BF16),
             pltpu.VMEM(square, BF16),
             pltpu.VMEM((packed.shape[0], size), F32),
+            pltpu.SemaphoreType.DMA((5,)),
         ],
-        compiler_params=pltpu.CompilerParams(vmem_limit_bytes=40 << 20),
+        compiler_params=pltpu.CompilerParams(vmem_limit_bytes=60 << 20),
         name="refine_and_scan",
     )(start, s_hi, s_lo, packed, initial_mean.reshape(1, size))
     if kept_width == width:

time: 39.2 us -> 34.4 us (0.88)
  local copies, waits for them, and re-layouts: 5.1 us -> 0 us
  Pallas kernels: 33.8 us -> 34.2 us
    unnamed x12 -> x0, local copies, waits for them, and re-layouts: 5.1 us -> none
    pallas_call x1, Pallas kernels: 25 us -> 26.5 us  [body(): pl.pallas_call(scan_kernel, out_shape=jax.ShapeDtypeStruct((frames, kept_...]
    pallas_call x1, Pallas kernels: 8.77 us -> 7.71 us  [share_and_build(): pl.pallas_call(share_and_build_kernel, out_shape=(jax.ShapeDtypeStruct(sq...]
where the time goes in v2:
time: 34.4 us; the launch traced here: 34.2 us
  Pallas kernels  34.2 us (99%)
    pallas_call x1, Pallas kernels, body(): pl.pallas_call(scan_kernel, out_shape=jax.ShapeDtypeStruct((frames, kept_...  26.5 us
    pallas_call x1, Pallas kernels, share_and_build(): pl.pallas_call(share_and_build_kernel, out_shape=(jax.ShapeDtypeStruct(sq...  7.71 us

profile of v2, /device:TPU:27, one launch (start us, length us, event | category | flops | bytes accessed | tf_op | source)
XLA Modules:
  0.0 34.2 jit_solution(298817248590133050)
XLA Ops:
  0.0 7.7 %share_and_build.1 = (f32[512,512]{1,0:T(8,128)}, bf16[512,512]{1,0:T(8,128)(2,1)}, bf16[512,512]{1,0:T(8,128)(2,1)}, f32[4,32,1024]{2,1,0:T(8,128)}) custom-call(f32[32,512]{1,0:T(8,128)} %observations_hbm.1, f32[32,512]{1,0:T(8,128)} %gains_hbm.1, s32[32,512]{1,0:T(8,128)} %observed_hbm.1, s32[8,8]{1,0:T(8,128)} %pattern_hbm.1, f32[512,512]{1,0:T(8,128)} %transition_hbm.1), custom_call_target="tpu_custom_call" | custom-call | tf_op jit(solution)/shard_map/share_and_build/pallas_call | solution.py:165
  7.7 26.5 %refine_and_scan.1 = f32[32,128]{1,0:T(8,128)} custom-call(f32[512,512]{1,0:T(8,128)} %get-tuple-element.9.y_hbm, bf16[512,512]{1,0:T(8,128)(2,1)} %get-tuple-element.10.s_hi_hbm, bf16[512,512]{1,0:T(8,128)(2,1)} %get-tuple-element.11.s_lo_hbm, f32[128,1024]{1,0:T(8,128)} %bitcast.2, f32[1,512]{1,0:T(1,128)} %bitcast.3), custom_call_target="tpu_custom_call" | custom-call | tf_op jit(solution)/shard_map/refine_and_scan/pallas_call | solution.py:294

commit v3 on v2

--- a/solution.py
+++ b/solution.py
@@ -226,18 +226,25 @@
     def refine(carry):
         step, unused = carry
         r_hi, r_lo = split(r_ref[...])
-        prod = dot1(y_hi[...], r_lo) + dot1(y_lo[...], r_hi)
-        ft_ref[...] += prod + dot1(y_hi[...], r_hi)
+        ft_ref[...] += dot1(y_hi[...], r_hi)
+
+        @pl.when(step > 0)
+        def _():
+            ft_ref[...] += dot1(y_hi[...], r_lo) + dot1(y_lo[...], r_hi)
+
         return step + 1, residual()
 
-    lax.while_loop(unfinished, refine, (0, jnp.where(good, first, 1e9)))
+    lax.while_loop(
+        unfinished, refine, (jnp.where(good, 0, 1), jnp.where(good, first, 1e9))
+    )
     last = ft_ref[...] + dot1(y_hi[...], r_ref[...].astype(BF16))
     ft_ref[...] = 2.0 * last - eye()
 
 
 def scan_kernel(
     y_hbm, s_hi_hbm, s_lo_hbm, frames_hbm, start_hbm, out_ref,
-    ft_ref, s_hi, s_lo, frames_ref, start_ref, r_ref, y_hi, y_lo, kept, load_sem,
+    ft_ref, s_hi, s_lo, frames_ref, start_ref, r_ref, y_hi, y_lo, kept,
+    f_ref, moved_drive, damp_parts, columns, load_sem,
 ):
     loads = []
     for place, (source, target) in enumerate((
@@ -256,30 +263,76 @@
         load.wait()
     size = ft_ref.shape[0]
     frames, width = out_ref.shape
+    tiles = size // 128
+    groups = size // 8
     mine = lax.axis_index("tm")
     offset = 0 if width == size else lax.axis_index("state") * width
-
-    def step(t, row):
+    f_ref[...] = ft_ref[...].T
+
+    ft_hi, ft_lo = split(ft_ref[...])
+    drive_hi, drive_lo = split(frames_ref[:, size:])
+    moved_drive[...] = (dot1(drive_hi, ft_lo) + dot1(drive_lo, ft_hi)) + dot1(drive_hi, ft_hi)
+
+    def finish(acc, t, extra):
+        moved = jnp.sum(acc[0] + acc[1], axis=0, keepdims=True) + extra
+        return frames_ref[pl.ds(t, 1), :size] * moved + frames_ref[pl.ds(t, 1), size:]
+
+    def earlier_chunk(chunk, row):
+        base = pl.multiple_of(chunk * frames, frames)
+        damp = frames_ref[pl.ds(base, frames), :size].T
+        high, low = split(damp)
+        least = (damp - high.astype(F32) - low.astype(F32)).astype(BF16)
+        for place, part in enumerate((high, low, least)):
+            damp_parts[:, frames * place : frames * (place + 1)] = part
+        at = lax.broadcasted_iota(jnp.int32, (3 * frames, 256), 0)
+        lane = lax.broadcasted_iota(jnp.int32, (3 * frames, 256), 1)
+
+        def spread_damp(four):
+            wanted = 4 * four + 2 * (lane // 128)
+            pick = (lax.rem(at, frames) == wanted).astype(BF16)
+            return dot1(damp_parts[...], pick)
+
+        def pair(t, row, now, half):
+            spread = jnp.broadcast_to(row, (8, size))
+            acc = [jnp.zeros((8, size), F32), jnp.zeros((8, size), F32)]
+            for group in range(groups):
+                rows = slice(8 * group, 8 * group + 8)
+                part = f_ref[rows, :] * spread
+                part = sum(part[:, 128 * k : 128 * k + 128] for k in range(tiles))
+                column = jnp.broadcast_to(jnp.sum(part, axis=1, keepdims=True), (8, 128))
+                column = column * columns[now, rows, 128 * half : 128 * half + 128]
+                acc[group % 2] += ft_ref[rows, :] * jnp.concatenate([column] * tiles, 1)
+            return finish(acc, t + 1, moved_drive[pl.ds(t, 1), :])
+
+        def fours(four, row):
+            now = lax.rem(four, 2)
+            row = pair(base + 4 * four, row, now, 0)
+            columns[1 - now] = spread_damp(four + 1)
+            return pair(base + 4 * four + 2, row, now, 1)
+
+        columns[0] = spread_damp(0)
+        return lax.fori_loop(0, frames // 4, fours, row)
+
+    row = lax.fori_loop(0, mine, earlier_chunk, start_ref[...])
+
+    def step(local, row):
         acc = [jnp.zeros((8, size), F32), jnp.zeros((8, size), F32)]
-        for tile in range(size // 128):
+        for tile in range(tiles):
             piece = row[:, 128 * tile : 128 * tile + 128]
             column = jnp.broadcast_to(piece, (128, 128)).T
             for group in range(16):
                 at = 128 * tile + 8 * group
-                spread = jnp.concatenate([column[8 * group : 8 * group + 8]] * (size // 128), 1)
+                spread = jnp.concatenate([column[8 * group : 8 * group + 8]] * tiles, 1)
                 acc[group % 2] += ft_ref[at : at + 8, :] * spread
-        moved = jnp.sum(acc[0] + acc[1], axis=0, keepdims=True)
-        damp = frames_ref[pl.ds(t, 1), :size]
-        drive = frames_ref[pl.ds(t, 1), size:]
-        row = damp * moved + drive
-        kept[pl.ds(t, 1), :] = row
+        row = finish(acc, mine * frames + local, 0.0)
+        kept[pl.ds(local, 1), :] = row
         return row
 
-    lax.fori_loop(0, (mine + 1) * frames, step, start_ref[...])
-    out_ref[...] = kept[
-        pl.ds(pl.multiple_of(mine * frames, frames), frames),
-        pl.ds(0, size) if width == size else pl.ds(pl.multiple_of(offset, width), width),
-    ]
+    lax.fori_loop(0, frames, step, row)
+    if width == size:
+        out_ref[...] = kept[...]
+    else:
+        out_ref[...] = kept[:, pl.ds(pl.multiple_of(offset, width), width)]
 
 
 def body(observations, gains, observed, pattern, transition, initial_mean):
@@ -305,7 +358,11 @@
             pltpu.VMEM(square, F32),
             pltpu.VMEM(square, BF16),
             pltpu.VMEM(square, BF16),
+            pltpu.VMEM((frames, size), F32),
+            pltpu.VMEM(square, F32),
             pltpu.VMEM((packed.shape[0], size), F32),
+            pltpu.VMEM((size, 3 * frames), BF16),
+            pltpu.VMEM((2, size, 256), F32),
             pltpu.SemaphoreType.DMA((5,)),
         ],
         compiler_params=pltpu.CompilerParams(vmem_limit_bytes=60 << 20),

time: 34.4 us -> 29.5 us (0.86)
  Pallas kernels: 34.2 us -> 29.3 us
    pallas_call x1, Pallas kernels: 26.5 us -> 21.6 us  [body(): pl.pallas_call(scan_kernel, out_shape=jax.ShapeDtypeStruct((frames, kept_...]
where the time goes in v3:
time: 29.5 us; the launch traced here: 29.3 us
  Pallas kernels  29.3 us (99%)
    pallas_call x1, Pallas kernels, body(): pl.pallas_call(scan_kernel, out_shape=jax.ShapeDtypeStruct((frames, kept_...  21.6 us
    pallas_call x1, Pallas kernels, share_and_build(): pl.pallas_call(share_and_build_kernel, out_shape=(jax.ShapeDtypeStruct(sq...  7.71 us

profile of v3, /device:TPU:27, one launch (start us, length us, event | category | flops | bytes accessed | tf_op | source)
XLA Modules:
  0.0 29.3 jit_solution(5140151620137184319)
XLA Ops:
  0.0 7.7 %share_and_build.1 = (f32[512,512]{1,0:T(8,128)}, bf16[512,512]{1,0:T(8,128)(2,1)}, bf16[512,512]{1,0:T(8,128)(2,1)}, f32[4,32,1024]{2,1,0:T(8,128)}) custom-call(f32[32,512]{1,0:T(8,128)} %observations_hbm.1, f32[32,512]{1,0:T(8,128)} %gains_hbm.1, s32[32,512]{1,0:T(8,128)} %observed_hbm.1, s32[8,8]{1,0:T(8,128)} %pattern_hbm.1, f32[512,512]{1,0:T(8,128)} %transition_hbm.1), custom_call_target="tpu_custom_call" | custom-call | tf_op jit(solution)/shard_map/share_and_build/pallas_call | solution.py:165
  7.7 21.6 %refine_and_scan.1 = f32[32,128]{1,0:T(8,128)} custom-call(f32[512,512]{1,0:T(8,128)} %get-tuple-element.9.y_hbm, bf16[512,512]{1,0:T(8,128)(2,1)} %get-tuple-element.10.s_hi_hbm, bf16[512,512]{1,0:T(8,128)(2,1)} %get-tuple-element.11.s_lo_hbm, f32[128,1024]{1,0:T(8,128)} %bitcast.2, f32[1,512]{1,0:T(1,128)} %bitcast.3), custom_call_target="tpu_custom_call" | custom-call | tf_op jit(solution)/shard_map/refine_and_scan/pallas_call | solution.py:347

commit v4 on v3

--- a/solution.py
+++ b/solution.py
@@ -244,7 +244,7 @@
 def scan_kernel(
     y_hbm, s_hi_hbm, s_lo_hbm, frames_hbm, start_hbm, out_ref,
     ft_ref, s_hi, s_lo, frames_ref, start_ref, r_ref, y_hi, y_lo, kept,
-    f_ref, moved_drive, damp_parts, columns, load_sem,
+    f_ref, moved_drive, before, damp_parts, columns, load_sem,
 ):
     loads = []
     for place, (source, target) in enumerate((
@@ -277,7 +277,7 @@
         moved = jnp.sum(acc[0] + acc[1], axis=0, keepdims=True) + extra
         return frames_ref[pl.ds(t, 1), :size] * moved + frames_ref[pl.ds(t, 1), size:]
 
-    def earlier_chunk(chunk, row):
+    def one_chunk(chunk, row):
         base = pl.multiple_of(chunk * frames, frames)
         damp = frames_ref[pl.ds(base, frames), :size].T
         high, low = split(damp)
@@ -293,6 +293,7 @@
             return dot1(damp_parts[...], pick)
 
         def pair(t, row, now, half):
+            before[pl.ds((t - base) // 2, 1), :] = row
             spread = jnp.broadcast_to(row, (8, size))
             acc = [jnp.zeros((8, size), F32), jnp.zeros((8, size), F32)]
             for group in range(groups):
@@ -302,7 +303,9 @@
                 column = jnp.broadcast_to(jnp.sum(part, axis=1, keepdims=True), (8, 128))
                 column = column * columns[now, rows, 128 * half : 128 * half + 128]
                 acc[group % 2] += ft_ref[rows, :] * jnp.concatenate([column] * tiles, 1)
-            return finish(acc, t + 1, moved_drive[pl.ds(t, 1), :])
+            row = finish(acc, t + 1, moved_drive[pl.ds(t, 1), :])
+            kept[pl.ds(t - base + 1, 1), :] = row
+            return row
 
         def fours(four, row):
             now = lax.rem(four, 2)
@@ -313,22 +316,16 @@
         columns[0] = spread_damp(0)
         return lax.fori_loop(0, frames // 4, fours, row)
 
-    row = lax.fori_loop(0, mine, earlier_chunk, start_ref[...])
-
-    def step(local, row):
-        acc = [jnp.zeros((8, size), F32), jnp.zeros((8, size), F32)]
-        for tile in range(tiles):
-            piece = row[:, 128 * tile : 128 * tile + 128]
-            column = jnp.broadcast_to(piece, (128, 128)).T
-            for group in range(16):
-                at = 128 * tile + 8 * group
-                spread = jnp.concatenate([column[8 * group : 8 * group + 8]] * tiles, 1)
-                acc[group % 2] += ft_ref[at : at + 8, :] * spread
-        row = finish(acc, mine * frames + local, 0.0)
-        kept[pl.ds(local, 1), :] = row
-        return row
-
-    lax.fori_loop(0, frames, step, row)
+    lax.fori_loop(0, mine + 1, one_chunk, start_ref[...])
+
+    high, low = split(before[...])
+    before[...] = (dot1(high, ft_lo) + dot1(low, ft_hi)) + dot1(high, ft_hi)
+    for place in range(frames // 2):
+        at = mine * frames + 2 * place
+        kept[2 * place : 2 * place + 1, :] = (
+            frames_ref[pl.ds(at, 1), :size] * before[place : place + 1, :]
+            + frames_ref[pl.ds(at, 1), size:]
+        )
     if width == size:
         out_ref[...] = kept[...]
     else:
@@ -361,6 +358,7 @@
             pltpu.VMEM((frames, size), F32),
             pltpu.VMEM(square, F32),
             pltpu.VMEM((packed.shape[0], size), F32),
+            pltpu.VMEM((frames // 2, size), F32),
             pltpu.VMEM((size, 3 * frames), BF16),
             pltpu.VMEM((2, size, 256), F32),
             pltpu.SemaphoreType.DMA((5,)),

time: 29.5 us -> 28.2 us (0.956)
  Pallas kernels: 29.3 us -> 28 us
    pallas_call x1, Pallas kernels: 21.6 us -> 20.3 us  [body(): pl.pallas_call(scan_kernel, out_shape=jax.ShapeDtypeStruct((frames, kept_...]
where the time goes in v4:
time: 28.2 us; the launch traced here: 28 us
  Pallas kernels  28 us (99%)
    pallas_call x1, Pallas kernels, body(): pl.pallas_call(scan_kernel, out_shape=jax.ShapeDtypeStruct((frames, kept_...  20.3 us
    pallas_call x1, Pallas kernels, share_and_build(): pl.pallas_call(share_and_build_kernel, out_shape=(jax.ShapeDtypeStruct(sq...  7.71 us

profile of v4, /device:TPU:27, one launch (start us, length us, event | category | flops | bytes accessed | tf_op | source)
XLA Modules:
  0.0 28.0 jit_solution(4165632321587957135)
XLA Ops:
  0.0 7.7 %share_and_build.1 = (f32[512,512]{1,0:T(8,128)}, bf16[512,512]{1,0:T(8,128)(2,1)}, bf16[512,512]{1,0:T(8,128)(2,1)}, f32[4,32,1024]{2,1,0:T(8,128)}) custom-call(f32[32,512]{1,0:T(8,128)} %observations_hbm.1, f32[32,512]{1,0:T(8,128)} %gains_hbm.1, s32[32,512]{1,0:T(8,128)} %observed_hbm.1, s32[8,8]{1,0:T(8,128)} %pattern_hbm.1, f32[512,512]{1,0:T(8,128)} %transition_hbm.1), custom_call_target="tpu_custom_call" | custom-call | tf_op jit(solution)/shard_map/share_and_build/pallas_call | solution.py:165
  7.7 20.3 %refine_and_scan.1 = f32[32,128]{1,0:T(8,128)} custom-call(f32[512,512]{1,0:T(8,128)} %get-tuple-element.9.y_hbm, bf16[512,512]{1,0:T(8,128)(2,1)} %get-tuple-element.10.s_hi_hbm, bf16[512,512]{1,0:T(8,128)(2,1)} %get-tuple-element.11.s_lo_hbm, f32[128,1024]{1,0:T(8,128)} %bitcast.2, f32[1,512]{1,0:T(1,128)} %bitcast.3), custom_call_target="tpu_custom_call" | custom-call | tf_op jit(solution)/shard_map/refine_and_scan/pallas_call | solution.py:344
